TPU v7x, 256 devices: a whole 4x4x8 slice. The times are simulated.
256 devices in a mesh: row: 8 (over x, core), col: 32 (over z, y).
Axes of the slice: x: 4, y: 4, z: 8, core: 2. Of those that a mesh axis runs over, the one named last changes fastest.
Arguments:
- images: bfloat16 [24576, 768], P(('row', 'col')), may hold values from -16 to 16
- texts: bfloat16 [24576, 768], P(('row', 'col')), may hold values from -16 to 16
- logit_scale: float32 [1], replicated, may hold values from 0.05 to 0.15
Outputs:
- loss: float32 [1], replicated
- grad_images: float32 [24576, 768], P(('row', 'col'))
- grad_texts: float32 [24576, 768], P(('row', 'col'))
All inputs are finite; a program needn't handle non-finite values.
Results may differ from a plain program's by a relative error of at most 0.002.
Values may be sent and summed in bfloat16 or wider, within the bound.
A program may use at most 192 MiB of HBM per device.

v0:
```python
import jax
import jax.numpy as jnp
from jax import lax
from jax.sharding import PartitionSpec as P


def pair_scores(left, right, scale):
    return scale * lax.dot_general(
        left, right, (((1,), (1,)), ((), ())), preferred_element_type=jnp.float32
    )


def local(images, texts, logit_scale):
    scale = logit_scale[0]
    pair_rows = images.shape[0]
    n_row = lax.axis_size("row")
    n_col = lax.axis_size("col")
    col_place = lax.axis_index("col")
    row_place = lax.axis_index("row")
    text_col = lax.all_gather(texts, "row", axis=0, tiled=True)
    image_row = lax.all_gather(images, "col", axis=0, tiled=True)
    scores = pair_scores(image_row, text_col, scale)
    row_local = jnp.max(scores, axis=1)
    col_local = jnp.max(scores, axis=0)
    row_top = lax.pmax(row_local, "col")
    row_sum = lax.psum(jnp.sum(jnp.exp(scores - row_top[:, None]), axis=1), "col")
    col_top = lax.pmax(col_local, "row")
    col_sum = lax.psum(jnp.sum(jnp.exp(scores - col_top[None, :]), axis=0), "row")
    lse_img = row_top + jnp.log(row_sum)
    lse_txt = col_top + jnp.log(col_sum)
    weights = (
        (jnp.exp(scores - lse_img[:, None]) + jnp.exp(scores - lse_txt[None, :])) * (scale * 0.5)
    ).astype(jnp.bfloat16)
    piece = weights
    image_sum = lax.psum_scatter(
        jnp.dot(piece, text_col, preferred_element_type=jnp.float32),
        "col",
        scatter_dimension=0,
        tiled=True,
    )
    piece = weights
    text_sum = lax.psum_scatter(
        lax.dot_general(
            piece, image_row, (((0,), (0,)), ((), ())), preferred_element_type=jnp.float32
        ),
        "row",
        scatter_dimension=0,
        tiled=True,
    )
    own_img = lax.dynamic_slice_in_dim(lse_img, col_place * pair_rows, pair_rows, 0)
    own_txt = lax.dynamic_slice_in_dim(lse_txt, row_place * pair_rows, pair_rows, 0)
    images_f = images.astype(jnp.float32)
    texts_f = texts.astype(jnp.float32)
    matched = scale * jnp.sum(images_f * texts_f, axis=1)
    part_loss = jnp.sum(own_img) + jnp.sum(own_txt) - 2.0 * jnp.sum(matched)
    all_pairs = pair_rows * n_row * n_col
    loss = lax.psum(part_loss, ("row", "col")) / (2.0 * all_pairs)
    grad_images = image_sum - scale * texts_f
    grad_texts = text_sum - scale * images_f
    return (loss.reshape(1), grad_images, grad_texts)


def solution(mesh):
    placed = (P(("row", "col"), None), P(("row", "col"), None), P())
    return jax.shard_map(
        local,
        mesh=mesh,
        in_specs=placed,
        out_specs=(P(), P(("row", "col"), None), P(("row", "col"), None)),
        check_vma=False,
    )
```

profile of v0, /device:TPU:1, one launch (start us, length us, event | category | flops | bytes accessed | tf_op | source)
XLA Modules:
  0.0 813.8 jit_solution(93282084000853698)
XLA Ops:
  7.2 0.7 all-gather.5.cloned.1.call-update
  7.9 0.0 all-gather.3.cloned.1.call-start
  7.9 0.7 all-gather.3.cloned.1.call-update
  8.6 0.0 reduce-scatter.5.cloned.1.call-start
  9.3 30.9 %all-gather.5.cloned.1.call-done = bf16[768,768]{1,0:T(8,128)(2,1)} async-done(((bf16[96,768]{1,0:T(8,128)(2,1)}), bf16[768,768]{1,0:T(8,128)(2,1)}) %all-gather.5.cloned.1.call-update) | async-done | bytes 1179664 | tf_op jit(solution)/shard_map/all_gather | solution.py:20
  40.2 83.1 %all-gather.3.cloned.1.call-done = bf16[3072,768]{1,0:T(8,128)(2,1)} async-done(((bf16[96,768]{1,0:T(8,128)(2,1)}), bf16[3072,768]{1,0:T(8,128)(2,1)}) %all-gather.3.cloned.1.call-update) | async-done | bytes 4718608 | tf_op jit(solution)/shard_map/all_gather | solution.py:21
  123.4 10.4 %multiply_reduce_fusion = (f32[768]{0:T(1024)S(1)}, f32[3072]{0:T(1024)S(1)}, f32[3072,768]{1,0:T(8,128)}) fusion(f32[]{:T(128)} %bitcast.13, bf16[3072,768]{1,0:T(8,128)(2,1)} %all-gather.3.cloned.1.call-done, bf16[768,768]{1,0:T(8,128)(2,1)} %all-gather.5.cloned.1.call-done), kind=kOutput, calls=%fused_computation.3 | convolution fusion | flops 3630952704 | bytes 15350788 | tf_op jit(solution)/shard_map/dot_general | solution.py:8
  133.8 111.9 %pmax.14 = f32[3072]{0:T(1024)S(1)} all-reduce(f32[3072]{0:T(1024)S(1)} %get-tuple-element.6), channel_id=1, replica_groups=mesh['row'=8,'col'=32] {'col'}, use_global_device_ids=true, to_apply=%region_1.0 | all-reduce | flops 3072 | bytes 24576 | tf_op jit(solution)/shard_map/pmax | solution.py:25
  245.6 43.7 %pmax.15 = f32[768]{0:T(1024)S(1)} all-reduce(f32[768]{0:T(1024)S(1)} %get-tuple-element.5), channel_id=1, replica_groups=mesh['row'=8,'col'=32] {'row'}, use_global_device_ids=true, to_apply=%region_6.0 | all-reduce | flops 768 | bytes 6144 | tf_op jit(solution)/shard_map/pmax | solution.py:27
  289.3 5.9 exponential_reduce_fusion
  295.3 12.4 %psum.22 = f32[768]{0:T(1024)S(1)} all-reduce(f32[768]{0:T(1024)S(1)} %get-tuple-element.3), channel_id=1, replica_groups=mesh['row'=8,'col'=32] {'row'}, use_global_device_ids=true, to_apply=%region_8.0 | all-reduce | flops 768 | bytes 6144 | tf_op jit(solution)/shard_map/psum | solution.py:28
  307.7 109.9 %psum.21 = f32[3072]{0:T(1024)S(1)} all-reduce(f32[3072]{0:T(1024)S(1)} %get-tuple-element.4), channel_id=1, replica_groups=mesh['row'=8,'col'=32] {'col'}, use_global_device_ids=true, to_apply=%region_3.0 | all-reduce | flops 3072 | bytes 24576 | tf_op jit(solution)/shard_map/psum | solution.py:26
  417.6 5.8 multiply_convert_fusion
  423.4 2.2 copy-done
  425.6 7.8 fusion.4
  433.4 0.2 reduce-scatter.3.cloned.1.call-start
  433.7 8.6 %fusion.3 = f32[3072,768]{1,0:T(8,128)} fusion(bf16[3072,768]{1,0:T(8,128)(2,1)} %copy-done, bf16[768,768]{1,0:T(8,128)(2,1)S(1)} %copy-done.3), kind=kOutput, calls=%fused_computation.16 | convolution fusion | flops 3623878656 | bytes 15335424 | tf_op jit(solution)/shard_map/dot_general | solution.py:36
  442.3 0.7 dynamic-slice_reduce_fusion
  443.0 0.7 dynamic-slice_reduce_fusion.1
  445.0 44.3 %reduce-scatter.5.cloned.1.call-done = f32[96,768]{1,0:T(8,128)} async-done(((f32[768,768]{1,0:T(8,128)}), f32[96,768]{1,0:T(8,128)}) %reduce-scatter.5.cloned.1.call-update) | async-done | bytes 294928 | tf_op jit(solution)/shard_map/reduce_scatter | solution.py:42
  489.3 234.0 %reduce-scatter.3.cloned.1.call-done = f32[96,768]{1,0:T(8,128)} async-done(((f32[3072,768]{1,0:T(8,128)}), f32[96,768]{1,0:T(8,128)}) %reduce-scatter.3.cloned.1.call-update) | async-done | bytes 294928 | tf_op jit(solution)/shard_map/reduce_scatter | solution.py:35
  723.3 2.0 fusion
  725.3 0.7 multiply_reduce_fusion.2
  726.7 78.8 %psum.23 = f32[]{:T(128)} all-reduce(f32[]{:T(128)S(6)} %sub.45), channel_id=1, replica_groups=mesh['row'=8,'col'=32] {'row','col'}, use_global_device_ids=true, to_apply=%region_12.0 | all-reduce | flops 1 | bytes 8 | tf_op jit(solution)/shard_map/psum | solution.py:57
  (12 shorter events, 0.1 us)
Async XLA Ops:
  7.2 33.1 %all-gather.5.cloned.1.call-start = ((), (), s32[]{:S(2)}) async-start(), calls=%async_computation.3 | async-start | bytes 1327104 | tf_op jit(solution)/shard_map/all_gather | solution.py:20
  7.9 115.5 %all-gather.3.cloned.1.call-start = ((), (), s32[]{:S(2)}) async-start(), calls=%async_computation.2 | async-start | bytes 4866048 | tf_op jit(solution)/shard_map/all_gather | solution.py:21
  8.6 480.7 %reduce-scatter.5.cloned.1.call-start = ((), (), s32[]{:S(2)}) async-start(), calls=%async_computation.5 | async-start | bytes 2654208 | tf_op jit(solution)/shard_map/reduce_scatter | solution.py:42
  423.4 2.2 copy-start
  425.6 8.0 copy-start.3
  433.4 289.8 %reduce-scatter.3.cloned.1.call-start = ((), (), s32[]{:S(2)}) async-start(), calls=%async_computation.4 | async-start | bytes 9732096 | tf_op jit(solution)/shard_map/reduce_scatter | solution.py:35
  442.3 281.0 %copy-start.1 = (bf16[96,768]{1,0:T(8,128)(2,1)S(1)}, bf16[96,768]{1,0:T(8,128)(2,1)}, u32[]{:S(2)}) copy-start(bf16[96,768]{1,0:T(8,128)(2,1)} %param.4) | copy-start | bytes 442372
  442.3 281.0 %copy-start.2 = (bf16[96,768]{1,0:T(8,128)(2,1)S(1)}, bf16[96,768]{1,0:T(8,128)(2,1)}, u32[]{:S(2)}) copy-start(bf16[96,768]{1,0:T(8,128)(2,1)} %param.3) | copy-start | bytes 442372
Sparse Core Ops, SparseCore 0:
  9.8 30.3 all-gather.4
  42.8 80.4 all-gather.2
  433.6 55.6 reduce-scatter.4
  493.2 230.0 reduce-scatter.2
where the time goes:
time: 814 us
  waiting for transfers between devices  394 us (48%)
  blocking collectives  357 us (44%)
  matrix products  26.8 us (3%)
  between operations  18.2 us (2%)
  other arithmetic  15.8 us (2%)
    reduce_scatter x1, waiting for transfers between devices, local(): lax.psum_scatter(jnp.dot(piece, text_col, preferred_element_type=jnp.floa...  234 us
    pmax x1, blocking collectives, local(): row_top = lax.pmax(row_local, 'col')  112 us
    psum x1, blocking collectives, local(): lax.psum(jnp.sum(jnp.exp(scores - row_top[:, None]), axis=1), 'col')  110 us
    all_gather x1, waiting for transfers between devices, local(): image_row = lax.all_gather(images, 'col', axis=0, tiled=True)  83.1 us
    psum x1, blocking collectives, local(): loss = lax.psum(part_loss, ('row', 'col')) / (2.0 * all_pairs)  78.8 us
    reduce_scatter x1, waiting for transfers between devices, local(): lax.psum_scatter(lax.dot_general(piece, image_row, (((0,), (0,)), ((), ()...  44.3 us
    pmax x1, blocking collectives, local(): col_top = lax.pmax(col_local, 'row')  43.7 us
    all_gather x1, waiting for transfers between devices, local(): text_col = lax.all_gather(texts, 'row', axis=0, tiled=True)  30.9 us
  transfers between devices with their start and end apart: 4, of which 4 were waited for; matrix products, arithmetic and copies ran while one was open for 1% of the time, Pallas kernels for 0%

commit v1 on v0

v1 whole, which is shorter than its diff:
```python
import functools
import math

import jax
import jax.numpy as jnp
from jax import lax
from jax.experimental import pallas as pl
from jax.experimental.pallas import tpu as pltpu
from jax.sharding import PartitionSpec as P

MESH = pl.DeviceIdType.MESH
F32 = jnp.float32
BF16 = jnp.bfloat16
NT = (((1,), (1,)), ((), ()))
NN = (((1,), (0,)), ((), ()))
TN = (((0,), (0,)), ((), ()))
LN2 = math.log(2.0)
NX, NY, NZ, NC = 4, 4, 8, 2
R = 96
HALF = R // 2
E = 768
SLOTS = 16
B = SLOTS * R
LANES = 128
GROUPS = B // LANES
TILE = 4 * R
CHUNK = 256

ZSTEPS = [0, 1, 7, 2, 6, 3, 5, 4]
ZPLACE = [ZSTEPS.index(d) for d in range(NZ)]
USTEPS = [0, 1, 3, 2]
UPLACE = [USTEPS.index(d) for d in range(4)]


def tree(f, parts):
    parts = list(parts)
    while len(parts) > 1:
        parts = [f(*parts[k:k + 2]) if k + 1 < len(parts) else parts[k] for k in range(0, len(parts), 2)]
    return parts[0]


def copy(src, dst, send, recv, to):
    return pltpu.make_async_remote_copy(
        src_ref=src, dst_ref=dst, send_sem=send, recv_sem=recv, device_id=to, device_id_type=MESH
    )


def rows_of(slot, count=R):
    return pl.ds(slot * R, count)


def lse_first(top, total=None):
    high = jnp.max(top, axis=0, keepdims=True)
    part = jnp.exp2(top - high)
    part = part if total is None else part * total
    return high + jnp.log2(jnp.sum(part, axis=0, keepdims=True))


def kernel(
    images, texts, scale_ref, loss_out, gi_out, gt_out,
    ibuf, tbuf, scores, weights, row_top, row_sum, col_part, col_shift,
    st_c, st_z, st_u, st_v, all_i, all_t, ls_c, ls_z, ls_x, ls_y,
    p_sib, p_in, p_own, p_send, p_recv, q_send, q_recv, q_own, r_recv,
    zi_s, zi_r, fi_s, fi_r, ti_s, ti_r, sc_s, sc_r, sz_s, sz_r, su_s, su_r, sv_s, sv_r,
    lc_s, lc_r, lz_s, lz_r, lx_s, lx_r, ly_s, ly_r, ps_s, ps_r, pz_s, pz_r, q_s, q_r, r_s, r_r,
):
    row, col = lax.axis_index("row"), lax.axis_index("col")
    x, c, z, y = row // NC, lax.rem(row, NC), col // NY, lax.rem(col, NY)
    u, v = x * (1 - c) + y * c, y * (1 - c) + x * c
    scale = scale_ref[0]

    def to(dx=0, dy=0, dz=0, dc=0):
        return (lax.rem(x + dx, NX) * NC + lax.rem(c + dc, NC), lax.rem(z + dz, NZ) * NY + lax.rem(y + dy, NY))

    def to_uv(du=0, dv=0):
        return to(dx=du * (1 - c) + dv * c, dy=dv * (1 - c) + du * c)

    sib = to(dc=1)
    started = []

    def launch(cp):
        cp.start()
        started.append(cp)
        return cp

    barrier = pltpu.get_barrier_semaphore()
    partners = [sib] + [to(dz=d) for d in ZSTEPS[1:]] + [to(dx=d) for d in USTEPS[1:]] + [to(dy=d) for d in USTEPS[1:]]
    for d in partners:
        pl.semaphore_signal(barrier, inc=1, device_id=d, device_id_type=MESH)
    pl.semaphore_wait(barrier, len(partners))

    forwards = []

    def z_copy(s, hop, h):
        k = (0 if s == 1 else 8) + (hop - 1) * 2 + h
        src = pl.ds(ZPLACE[(-s * (hop - 1)) % NZ] * R + h * HALF, HALF)
        dst = pl.ds(ZPLACE[(-s * hop) % NZ] * R + h * HALF, HALF)
        held = images.at[pl.ds(h * HALF, HALF)] if hop == 1 else ibuf.at[src]
        return copy(held, ibuf.at[dst], zi_s.at[k], zi_r.at[k], to(dz=s % NZ))

    def z_arrive(s, hop, h):
        z_copy(s, hop, h).wait_recv()
        if hop < 3 or (hop == 3 and h == (0 if s == 1 else 1)):
            launch(z_copy(s, hop + 1, h))
        k = (0 if s == 1 else 8) + (hop - 1) * 2 + h
        start = ZPLACE[(-s * hop) % NZ] * R + h * HALF
        forwards.append(launch(copy(
            ibuf.at[pl.ds(start, HALF)], ibuf.at[pl.ds(B // 2 + start, HALF)], fi_s.at[k], fi_r.at[k], sib
        )))

    def v_copy(s, hop):
        src, dst = UPLACE[(-s * (hop - 1)) % 4], UPLACE[(-s * hop) % 4]
        k = 2 if hop == 2 else (0 if s == 1 else 1)
        held = texts if hop == 1 else tbuf.at[rows_of(src)]
        return copy(held, tbuf.at[rows_of(dst)], ti_s.at[k], ti_r.at[k], to_uv(dv=s % 4))

    def u_copy(s, hop, pv):
        src, dst = 4 * UPLACE[(-s * (hop - 1)) % 4] + pv, 4 * UPLACE[(-s * hop) % 4] + pv
        k = 3 + pv * 3 + (2 if hop == 2 else (0 if s == 1 else 1))
        held = texts if hop == 1 and pv == 0 else tbuf.at[rows_of(src)]
        return copy(held, tbuf.at[rows_of(dst)], ti_s.at[k], ti_r.at[k], to_uv(du=s % 4))

    def v_arrive(s, hop):
        v_copy(s, hop).wait_recv()
        if hop == 1 and s == 1:
            launch(v_copy(1, 2))
        pv = UPLACE[(-s * hop) % 4]
        launch(u_copy(1, 1, pv))
        launch(u_copy(-1, 1, pv))

    def u_arrive(s, hop, pv):
        u_copy(s, hop, pv).wait_recv()
        if hop == 1 and s == (1 if pv % 2 == 0 else -1):
            launch(u_copy(s, 2, pv))

    for h in range(2):
        launch(z_copy(1, 1, h))
        launch(z_copy(-1, 1, h))
        if h == 0:
            launch(v_copy(1, 1))
            launch(v_copy(-1, 1))
    launch(u_copy(1, 1, 0))
    launch(u_copy(-1, 1, 0))
    forwards.append(launch(copy(images, ibuf.at[rows_of(8)], fi_s.at[16], fi_r.at[16], sib)))
    ibuf[rows_of(0)] = images[...]
    tbuf[rows_of(0)] = texts[...]
    z_events = [(s, hop, h) for hop in (1, 2, 3) for h in range(2) for s in (1, -1)] + [(1, 4, 0), (-1, 4, 1)]
    t_events = [
        (v_arrive, 1, 1), (v_arrive, -1, 1), (u_arrive, 1, 1, 0), (u_arrive, -1, 1, 0), (v_arrive, 1, 2),
        (u_arrive, 1, 1, 2), (u_arrive, -1, 1, 2), (u_arrive, 1, 1, 1), (u_arrive, -1, 1, 1), (u_arrive, 1, 2, 0),
        (u_arrive, 1, 1, 3), (u_arrive, -1, 1, 3), (u_arrive, 1, 2, 2), (u_arrive, -1, 2, 1), (u_arrive, -1, 2, 3),
    ]
    for n in range(15):
        if n < 14:
            z_arrive(*z_events[n])
        f, *what = t_events[n]
        f(*what)
    for cp in forwards:
        cp.wait_recv()

    scale2 = scale * (1.0 / LN2)

    @pl.loop(0, B // CHUNK)
    def _(t):
        r0 = pl.multiple_of(t * CHUNK, CHUNK)
        tile = scale2 * lax.dot_general(ibuf[pl.ds(r0, CHUNK), :], tbuf[...], NT, preferred_element_type=F32)
        scores[pl.ds(r0, CHUNK), :] = tile
        for r in range(0, CHUNK, 32):
            parts = [tile[r:r + 32, g * LANES:(g + 1) * LANES] for g in range(GROUPS)]
            top = tree(jnp.maximum, parts)
            row_top[pl.ds(r0 + r, 32), :] = top
            row_sum[pl.ds(r0 + r, 32), :] = tree(jnp.add, [jnp.exp2(w - top) for w in parts])
        r8 = pl.ds(pl.multiple_of(t * 8, 8), 8)
        for g in range(GROUPS):
            parts = [tile[r:r + 8, g * LANES:(g + 1) * LANES] for r in range(0, CHUNK, 8)]
            top = tree(jnp.maximum, parts)
            col_part[0, r8, g * LANES:(g + 1) * LANES] = top
            col_part[1, r8, g * LANES:(g + 1) * LANES] = tree(jnp.add, [jnp.exp2(w - top) for w in parts])

    def i_row(k):
        return lax.rem(c + k // NZ, NC) * NZ + lax.rem(z + ZSTEPS[k % NZ], NZ)

    def t_row(k):
        return lax.rem(u + USTEPS[k // 4], 4) * 4 + lax.rem(v + USTEPS[k % 4], 4)

    def spread(st, mine, steps, where, ss, rs):
        return [launch(copy(st.at[mine], st.at[mine], ss.at[k], rs.at[k], where(d))) for k, d in enumerate(steps)]

    def along_z(d):
        return to(dz=d)

    st_c[c] = jnp.zeros((SLOTS, LANES), F32)
    st_u[u] = jnp.zeros((SLOTS, LANES), F32)
    lse = lse_first(col_part[0], col_part[1])
    for k in range(SLOTS):
        st_u[u, pl.ds(t_row(k), 1), 0:R] = lse[:, k * R:(k + 1) * R]
    u_cps = spread(st_u, u, USTEPS[1:], lambda d: to_uv(du=d), su_s, su_r)
    lse = lse_first(row_top[...].T, row_sum[...].T)
    for k in range(SLOTS):
        st_c[c, pl.ds(i_row(k), 1), 0:R] = lse[:, k * R:(k + 1) * R]
    c_cp = launch(copy(st_c.at[c], st_c.at[c], sc_s.at[0], sc_r.at[0], sib))
    for cp in u_cps:
        cp.wait_recv()
    st_v[v] = lse_first(st_u[...])[0]
    v_cps = spread(st_v, v, USTEPS[1:], lambda d: to_uv(dv=d), sv_s, sv_r)
    c_cp.wait_recv()
    st_z[z] = lse_first(st_c[...])[0]
    z_cps = spread(st_z, z, ZSTEPS[1:], along_z, sz_s, sz_r)
    half = jnp.log2(jnp.full((1, LANES), scale * 0.5, F32))
    for cp in v_cps:
        cp.wait_recv()
    all_t[...] = lse_first(st_v[...])[0]
    for k in range(SLOTS):
        col_shift[0:1, k * R:(k + 1) * R] = (all_t[pl.ds(t_row(k), 1), :] - half)[:, 0:R]
    for cp in z_cps:
        cp.wait_recv()
    all_i[...] = lse_first(st_z[...])[0]
    for k in range(SLOTS):
        shift = jnp.broadcast_to(all_i[pl.ds(i_row(k), 1), :] - half, (LANES, LANES)).T
        row_top[rows_of(k), :] = shift[0:R]

    lane = lax.broadcasted_iota(jnp.int32, (1, LANES), 1)
    matched = images[...].astype(F32) * texts[...].astype(F32)
    matched = jnp.sum(matched, axis=0, keepdims=True)
    matched = tree(jnp.add, [matched[:, g * LANES:(g + 1) * LANES] for g in range(E // LANES)])
    own = all_i[pl.ds(i_row(0), 1), :] + all_t[pl.ds(t_row(0), 1), :]
    own = LN2 * jnp.where(lane < R, own, 0.0) - (2.0 * scale) * matched
    ls_c[c] = jnp.broadcast_to(own, (8, LANES))
    lc_cp = launch(copy(ls_c.at[c], ls_c.at[c], lc_s.at[0], lc_r.at[0], sib))

    def loss_z():
        lc_cp.wait_recv()
        ls_z[z] = ls_c[0] + ls_c[1]
        return spread(ls_z, z, ZSTEPS[1:], along_z, lz_s, lz_r)

    def loss_x(cps):
        for cp in cps:
            cp.wait_recv()
        ls_x[x] = functools.reduce(jnp.add, [ls_z[k] for k in range(NZ)])
        return spread(ls_x, x, USTEPS[1:], lambda d: to(dx=d), lx_s, lx_r)

    def loss_y(cps):
        for cp in cps:
            cp.wait_recv()
        ls_y[y] = functools.reduce(jnp.add, [ls_x[k] for k in range(NX)])
        return spread(ls_y, y, USTEPS[1:], lambda d: to(dy=d), ly_s, ly_r)

    def make_weights(first, count):
        @pl.loop(first // 64, (first + count) // 64)
        def _(t):
            rows = pl.ds(pl.multiple_of(t * 64, 64), 64)
            shift = row_top[rows, :]
            for g in range(GROUPS):
                cols = pl.ds(g * LANES, LANES)
                w = scores[rows, cols]
                w = jnp.exp2(w - shift) + jnp.exp2(w - col_shift[0:1, cols])
                weights[rows, cols] = w.astype(BF16)

    def p_tile(slot):
        return lax.dot_general(weights[rows_of(slot, TILE), :], tbuf[...], NN, preferred_element_type=F32)

    def sib_copy(h):
        rows = pl.ds(h * TILE, TILE)
        return copy(p_sib.at[rows], p_in.at[rows], ps_s.at[h], ps_r.at[h], sib)

    def do_sib(h):
        p_sib[pl.ds(h * TILE, TILE)] = p_tile(8 + 4 * h)
        launch(sib_copy(h))

    def p_copy(p):
        back = ZPLACE[-ZSTEPS[p] % NZ]
        return copy(p_send.at[rows_of(p)], p_recv.at[back], pz_s.at[p], pz_r.at[p], to(dz=ZSTEPS[p]))

    def do_own(h):
        rows = pl.ds(h * TILE, TILE)
        tile = p_tile(4 * h)
        sib_copy(h).wait_recv()
        tile = tile + p_in[rows]
        p_send[rows] = tile.astype(BF16)
        if h == 0:
            p_own[...] = tile[0:R]
        for p in range(4 * h + 3, 4 * h - 1, -1):
            if p:
                launch(p_copy(p))

    def q_copy(p):
        back = UPLACE[-USTEPS[p] % 4] - 1
        return copy(q_send.at[p - 1], q_recv.at[back], q_s.at[p - 1], q_r.at[p - 1], to_uv(du=USTEPS[p]))

    def do_q(p):
        tile = lax.dot_general(weights[:, rows_of(4 * p, TILE)], ibuf[...], TN, preferred_element_type=F32)
        if p:
            q_send[p - 1] = tile.astype(BF16)
            launch(q_copy(p))
        else:
            q_own[...] = tile

    def r_copy(p):
        back = UPLACE[-USTEPS[p] % 4] - 1
        return copy(q_own.at[rows_of(p)], r_recv.at[back], r_s.at[p - 1], r_r.at[p - 1], to_uv(dv=USTEPS[p]))

    make_weights(8 * R + TILE, TILE)
    loss_cps = loss_z()
    do_sib(1)
    make_weights(TILE, TILE)
    loss_cps = loss_x(loss_cps)
    do_own(1)
    make_weights(0, TILE)
    make_weights(8 * R, TILE)
    loss_cps = loss_y(loss_cps)
    do_q(3)
    do_q(1)
    do_q(2)
    do_sib(0)
    do_own(0)
    do_q(0)
    for cp in loss_cps:
        cp.wait_recv()
    total = functools.reduce(jnp.add, [ls_y[k] for k in range(NY)])
    loss_out[0] = jnp.sum(total[0:1]) * (1.0 / (2.0 * R * NX * NY * NZ * NC))

    for p in range(1, 4):
        q_copy(p).wait_recv()
    for p in (3, 1, 2, 0):
        @pl.loop(0, R // 32)
        def _(t, p=p):
            rows = pl.ds(pl.multiple_of(p * R + t * 32, 32), 32)
            q_own[rows] = functools.reduce(jnp.add, [q_recv[k, rows].astype(F32) for k in range(3)], q_own[rows])
        if p:
            launch(r_copy(p))
    for p in range(1, 8):
        p_copy(p).wait_recv()

    @pl.loop(0, R // 16)
    def _(t):
        rows = pl.ds(pl.multiple_of(t * 16, 16), 16)
        gi = p_own[rows] - scale * texts[rows].astype(F32)
        gi_out[rows] = functools.reduce(jnp.add, [p_recv[k, rows].astype(F32) for k in range(1, NZ)], gi)

    for p in range(1, 4):
        r_copy(p).wait_recv()

    @pl.loop(0, R // 16)
    def _(t):
        rows = pl.ds(pl.multiple_of(t * 16, 16), 16)
        gt = q_own[rows] - scale * images[rows].astype(F32)
        gt_out[rows] = functools.reduce(jnp.add, [r_recv[k, rows] for k in range(3)], gt)

    for cp in started:
        cp.wait_send()


def local(images, texts, logit_scale):
    vmem = pl.BlockSpec(memory_space=pltpu.VMEM)
    smem = pl.BlockSpec(memory_space=pltpu.SMEM)
    dma = pltpu.SemaphoreType.DMA
    scratch = [
        pltpu.VMEM((B, E), BF16), pltpu.VMEM((B, E), BF16), pltpu.VMEM((B, B), F32), pltpu.VMEM((B, B), BF16),
        pltpu.VMEM((B, LANES), F32), pltpu.VMEM((B, LANES), F32),
        pltpu.VMEM((2, 8 * (B // CHUNK), B), F32), pltpu.VMEM((8, B), F32),
    ]
    scratch += [pltpu.VMEM((n, SLOTS, LANES), F32) for n in (NC, NZ, 4, 4)]
    scratch += [pltpu.VMEM((SLOTS, LANES), F32)] * 2
    scratch += [pltpu.VMEM((n, 8, LANES), F32) for n in (NC, NZ, NX, NY)]
    scratch += [
        pltpu.VMEM((NZ * R, E), F32), pltpu.VMEM((NZ * R, E), F32), pltpu.VMEM((R, E), F32),
        pltpu.VMEM((NZ * R, E), BF16), pltpu.VMEM((NZ, R, E), BF16),
        pltpu.VMEM((3, TILE, E), BF16), pltpu.VMEM((3, TILE, E), BF16), pltpu.VMEM((TILE, E), F32),
        pltpu.VMEM((3, R, E), F32),
    ]
    for n in (16, 17, 15, 1, 7, 3, 3, 1, 7, 3, 3, 2, 8, 3, 3):
        scratch += [dma((n,)), dma((n,))]
    return pl.pallas_call(
        kernel,
        out_shape=(
            jax.ShapeDtypeStruct((1,), F32),
            jax.ShapeDtypeStruct((R, E), F32),
            jax.ShapeDtypeStruct((R, E), F32),
        ),
        in_specs=[vmem, vmem, smem],
        out_specs=(smem, vmem, vmem),
        scratch_shapes=scratch,
        compiler_params=pltpu.CompilerParams(
            collective_id=0, has_side_effects=True, vmem_limit_bytes=56 * 2**20
        ),
    )(images, texts, logit_scale)


def solution(mesh):
    placed = (P(("row", "col"), None), P(("row", "col"), None), P())
    return jax.shard_map(
        local,
        mesh=mesh,
        in_specs=placed,
        out_specs=(P(), P(("row", "col"), None), P(("row", "col"), None)),
        check_vma=False,
    )
```

time: 814 us -> 93.1 us (0.11)
  the two profiles are of different devices: /device:TPU:1 before, /device:TPU:2 now
where the time goes in v1:
time: 93.1 us; the launch traced here: 93 us
  Pallas kernels  87.4 us (94%)
  between operations  3.1 us (3%)
  local copies, waits for them, and re-layouts  2.46 us (3%)
    pallas_call x1, Pallas kernels, local(): pl.pallas_call(kernel, out_shape=(jax.ShapeDtypeStruct((1,), F32), jax.Sh...  87.4 us
    unnamed x4, local copies, waits for them, and re-layouts  2.46 us

profile of v1, /device:TPU:2, one launch (start us, length us, event | category | flops | bytes accessed | tf_op | source)
XLA Modules:
  0.0 93.0 jit_solution(4652134698649689910)
XLA Ops:
  1.3 87.4 %shard_map.58 = (f32[1]{0:T(128)}, f32[96,768]{1,0:T(8,128)}, f32[96,768]{1,0:T(8,128)}) custom-call(bf16[96,768]{1,0:T(8,128)(2,1)} %images.1, bf16[96,768]{1,0:T(8,128)(2,1)} %texts.1, f32[1]{0:T(128)S(6)} %copy.9.scale_ref), custom_call_target="tpu_custom_call" | custom-call | tf_op jit(solution)/shard_map/pallas_call | solution.py:373
  89.4 0.0 copy-start
  89.4 1.7 %copy.11 = f32[96,768]{1,0:T(8,128)} copy(f32[96,768]{1,0:T(8,128)} %get-tuple-element.7) | data formatting | bytes 589824
  91.1 0.0 copy-done
  91.1 0.7 copy.12
Async XLA Ops:
  89.4 1.8 %copy-start = (f32[96,768]{1,0:T(8,128)S(1)}, f32[96,768]{1,0:T(8,128)}, u32[]{:S(2)}) copy-start(f32[96,768]{1,0:T(8,128)} %get-tuple-element.8) | copy-start | bytes 884740
